TPU v7x, 256 devices: a whole 4x4x8 slice. The times are simulated.
256 devices in a mesh: ent: 32 (over y, x, core), rel: 8 (over z).
Axes of the slice: x: 4, y: 4, z: 8, core: 2. Of those that a mesh axis runs over, the one named last changes fastest.
Arguments:
- tile_vals: bfloat16 [32, 8, 64, 128, 128], P('ent', 'rel'), may hold values from -192 to 192
- tile_row: int32 [32, 8, 64], P('ent', 'rel'), may hold values from 0 to 3
- tile_rel: int32 [32, 8, 64], P('ent', 'rel'), may hold values from 0 to 1
- tile_src: int32 [32, 8, 64], P('ent', 'rel'), may hold values from 0 to 31
- needed: int32 [32, 8, 32, 1], P('ent', 'rel'), may hold values from 0 to 3
- factors: bfloat16 [16384, 256], P('ent'), may hold values from -6 to 6
- cores: bfloat16 [16, 256, 256], P('rel'), may hold values from -0.5 to 1.5
- basis: float32 [256, 256], replicated, may hold values from -1 to 1
- spectrum: float32 [256], replicated, may hold values from 100 to 1000
Outputs:
- new_factors: bfloat16 [16384, 256], P('ent')
- new_cores: float32 [16, 256, 256], P('rel')
Inputs may be any that keep to these rules, and one draw needn't show every extreme that they name: tile_src names the owner whose single requested block (slot 0 of `needed`) gives the tile's columns. `needed`: every request slot names a block.
All inputs are finite; a program needn't handle non-finite values.
Results may differ from a plain program's by a relative error of at most 0.0081.
Values may be sent and summed in bfloat16 or wider, within the bound.
A program may use at most 64 MiB of HBM per device.

v0:
```python
import jax
import jax.numpy as jnp
from jax import lax
from jax.sharding import PartitionSpec as P

ridge_shift = 1.0


def shards(tile_vals, tile_row, tile_rel, tile_src, needed, factors, cores, basis, spectrum):
    precise = lax.Precision.HIGHEST
    tile_data = tile_vals[0, 0]
    tile_rows = tile_row[0, 0]
    tile_rels = tile_rel[0, 0]
    sources = tile_src[0, 0]
    asked_rows = needed[0, 0]
    count_ent, slot_count = asked_rows.shape
    tile_edge = tile_data.shape[1]
    rank_width = factors.shape[1]
    rel_local = cores.shape[0]
    row_blocks = factors.shape[0] // tile_edge
    slot_total = count_ent * slot_count
    requests = lax.all_to_all(asked_rows, "ent", split_axis=0, concat_axis=0, tiled=True)

    def neighbour(slab_rows):
        whole_table = lax.all_gather(slab_rows, "ent", axis=0, tiled=True).reshape(
            count_ent, row_blocks, tile_edge, rank_width
        )
        fetched = whole_table[jnp.arange(count_ent)[:, None], asked_rows]
        return fetched.reshape(slot_total, tile_edge, rank_width)[sources]

    def grouped(part_data, key_ids, group_count):
        onehot = (key_ids[:, None] == jnp.arange(group_count, dtype=jnp.int32)[None, :]).astype(
            jnp.bfloat16
        )
        flat_part = part_data.reshape(part_data.shape[0], tile_edge * rank_width)
        return jnp.einsum(
            "tg,tx->gx", onehot, flat_part, preferred_element_type=jnp.float32
        ).astype(jnp.bfloat16)

    gathered_old = neighbour(factors)
    left_part = jnp.einsum(
        "tab,tbr->tar", tile_data, gathered_old, preferred_element_type=jnp.float32
    ).astype(jnp.bfloat16)
    forward = grouped(
        left_part, tile_rels * row_blocks + tile_rows, rel_local * row_blocks
    ).reshape(rel_local, row_blocks, tile_edge, rank_width)
    forward_term = jnp.einsum(
        "kbar,ksr->bas", forward, cores, preferred_element_type=jnp.float32
    ).reshape(-1, rank_width)
    own_blocks = factors.reshape(row_blocks, tile_edge, rank_width)
    right_part = jnp.einsum(
        "tab,tar->tbr", tile_data, own_blocks[tile_rows], preferred_element_type=jnp.float32
    ).astype(jnp.bfloat16)
    backward = grouped(right_part, sources * rel_local + tile_rels, slot_total * rel_local).reshape(
        slot_total, rel_local, tile_edge, rank_width
    )
    backward_term = jnp.einsum(
        "skbr,krq->sbq", backward, cores, preferred_element_type=jnp.float32
    ).reshape(count_ent, slot_count, tile_edge, rank_width)
    returned = lax.all_to_all(backward_term, "ent", split_axis=0, concat_axis=0, tiled=True)
    landing = (
        requests.reshape(1, slot_total) == jnp.arange(row_blocks, dtype=jnp.int32)[:, None]
    ).astype(jnp.float32)
    landed = jnp.dot(
        landing,
        returned.reshape(slot_total, tile_edge * rank_width),
        precision=precise,
        preferred_element_type=jnp.float32,
    ).reshape(-1, rank_width)
    gram_total = lax.psum(
        jnp.einsum("ar,as->rs", factors, factors, preferred_element_type=jnp.float32), "ent"
    )
    core_f32 = cores.astype(jnp.float32)
    system_part = jnp.einsum("kab,bc,kdc->ad", core_f32, gram_total, core_f32, precision=precise)
    system_part = system_part + jnp.einsum(
        "kba,bc,kcd->ad", core_f32, gram_total, core_f32, precision=precise
    )
    numerator, system = lax.psum((forward_term + landed, system_part), "rel")
    system = system + ridge_shift * jnp.eye(rank_width, dtype=jnp.float32)
    factor_low = jnp.linalg.cholesky(system)
    new_factors = jax.scipy.linalg.cho_solve((factor_low, True), numerator.T).T.astype(jnp.bfloat16)
    gathered_new = neighbour(new_factors)
    latest = jnp.einsum(
        "tab,tbr->tar", tile_data, gathered_new, preferred_element_type=jnp.float32
    ).astype(jnp.bfloat16)
    summed = grouped(latest, tile_rels * row_blocks + tile_rows, rel_local * row_blocks).reshape(
        rel_local, row_blocks, tile_edge, rank_width
    )
    core_part = jnp.einsum(
        "bar,kbas->krs",
        new_factors.reshape(row_blocks, tile_edge, rank_width),
        summed,
        preferred_element_type=jnp.float32,
    )
    weights = 1.0 / (spectrum[:, None] * spectrum[None, :] + ridge_shift)
    totals = lax.psum(core_part, "ent")
    rotated = jnp.einsum("ri,krs,sj->kij", basis, totals, basis, precision=precise)
    new_cores = jnp.einsum(
        "ir,krs,js->kij", basis, weights[None] * rotated, basis, precision=precise
    )
    return (new_factors, new_cores)


def solution(mesh):
    in_specs = (
        P("ent", "rel", None, None, None),
        P("ent", "rel", None),
        P("ent", "rel", None),
        P("ent", "rel", None),
        P("ent", "rel", None, None),
        P("ent", None),
        P("rel", None, None),
        P(),
        P(),
    )
    out_specs = (P("ent", None), P("rel", None, None))
    return jax.shard_map(shards, mesh=mesh, in_specs=in_specs, out_specs=out_specs, check_vma=False)
```

profile of v0, /device:TPU:1, one launch (start us, length us, event | category | flops | bytes accessed | tf_op | source)
XLA Modules:
  0.0 606.0 jit_solution(6752421999504624473)
XLA Ops:
  7.2 2.2 fusion.37
  9.5 0.7 all-gather.3.cloned.1.call-update
  10.2 1.3 copy.58
  11.5 8.6 %all-to-all-start = ((s32[32,1,1]{2,1,0:T(1,128)}), s32[32,1,1]{2,1,0:T(1,128)S(1)}, u32[]{:S(2)}, u32[]{:S(2)}) async-start(s32[32,1,1]{2,1,0:T(1,128)} %copy.58), calls=%async_computation | async-start | bytes 32768 | tf_op jit(solution)/shard_map/all_to_all | solution.py:22
  20.1 0.7 fusion.34
  20.8 2.7 gather_fusion.2
  23.5 5.5 convert_bitcast_fusion.1
  29.0 6.8 %copy.96 = bf16[8,8,128,256]{3,1,2,0:T(8,128)(2,1)} copy(bf16[8,8,128,256]{2,3,1,0:T(8,128)(2,1)} %bitcast.176) | data formatting | bytes 8388608
  35.9 3.6 convolution_convert_fusion
  39.5 1.1 copy.97
  40.6 3.2 convolution_bitcast_fusion
  43.8 7.6 %all-to-all-start.1 = ((f32[32,1,128,256]{3,2,1,0:T(8,128)}), f32[32,1,128,256]{3,2,1,0:T(8,128)}, u32[]{:S(2)}, u32[]{:S(2)}) async-start(f32[32,1,128,256]{3,2,1,0:T(8,128)} %convolution_bitcast_fusion), calls=%async_computation.1 | async-start | bytes 8388608 | tf_op jit(solution)/shard_map/all_to_all | solution.py:60
  51.3 0.5 all-reduce.10.cloned.1.call-start
  51.9 0.7 reduce.12
  52.6 100.5 %all-reduce.6.cloned.1.call-done = f32[256,256]{1,0:T(8,128)} async-done(((f32[256,256]{1,0:T(8,128)}), f32[256,256]{1,0:T(8,128)}) %all-reduce.6.cloned.1.call-update) | async-done | bytes 262160 | tf_op jit(solution)/shard_map/psum | solution.py:70
  153.1 1.4 fusion.17
  154.6 0.5 convolution_bitcast_fusion.3
  155.0 1.3 fusion.19
  156.4 1.2 fusion.5
  157.5 4.6 copy.98
  162.2 1.5 fusion.31
  163.7 0.4 reshape.241
  164.1 50.2 %all-gather.3.cloned.1.call-done = bf16[16384,256]{1,0:T(8,128)(2,1)} async-done(((bf16[512,256]{1,0:T(8,128)(2,1)}), bf16[16384,256]{1,0:T(8,128)(2,1)}) %all-gather.3.cloned.1.call-update) | async-done | bytes 8388624 | tf_op jit(solution)/shard_map/all_gather | solution.py:25
  214.2 5.4 gather_fusion
  219.7 4.4 gather_fusion.1
  224.0 5.5 convert_bitcast_fusion.2
  229.5 6.8 %copy.94 = bf16[8,8,128,256]{3,1,2,0:T(8,128)(2,1)} copy(bf16[8,8,128,256]{2,3,1,0:T(8,128)(2,1)} %bitcast.177) | data formatting | bytes 8388608
  236.3 2.9 convolution_convert_fusion.2
  239.4 1.1 fusion.4
  240.8 69.7 %all-reduce.10.cloned.1.call-done = (f32[256,512]{0,1:T(8,128)}, f32[256,256]{0,1:T(8,128)}) async-done(((f32[256,512]{0,1:T(8,128)}, f32[256,256]{0,1:T(8,128)}), (f32[256,512]{0,1:T(8,128)}, f32[256,256]{0,1:T(8,128)})) %all-reduce.10.cloned.1.call-update) | async-done | bytes 786448 | tf_op jit(solution)/shard_map/psum | solution.py:78
  310.5 1.0 convert_add_fusion
  311.6 1.0 fusion.16
  312.7 11.7 %cholesky.50 = f32[128,128]{1,0:T(8,128)S(1)} custom-call(f32[128,128]{1,0:T(8,128)S(1)} %cholesky.118), custom_call_target="Cholesky" | custom-call | tf_op jit(solution)/shard_map/jit(cholesky)/cholesky | solution.py:80
  324.4 9.8 %custom-call.18 = f32[1,128,128]{1,2,0:T(8,128)S(1)} custom-call(f32[1,128,128]{2,1,0:T(8,128)S(1)} %get-tuple-element.33), custom_call_target="InvertDiagBlocksLowerTriangular" | custom-call | tf_op jit(solution)/shard_map/jit(cholesky)/cholesky | solution.py:80
  334.5 0.3 convolution_subtract_fusion.2
  334.7 11.7 %cholesky.105 = f32[128,128]{1,0:T(8,128)S(1)} custom-call(f32[128,128]{1,0:T(8,128)S(1)} %convolution_subtract_fusion.2), custom_call_target="Cholesky" | custom-call | tf_op jit(solution)/shard_map/jit(cholesky)/cholesky | solution.py:80
  346.5 0.6 compare_reduce_fusion
  348.5 4.2 while.1
  348.7 0.6 fusion.70
  349.3 1.4 bitcast_dynamic-update-slice_fusion.2
  350.7 0.6 fusion.70
  351.3 1.4 bitcast_dynamic-update-slice_fusion.2
  352.7 19.7 %custom-call.19 = f32[2,128,128]{1,2,0:T(8,128)S(1)} custom-call(f32[2,128,128]{2,1,0:T(8,128)S(1)} %get-tuple-element.9), custom_call_target="InvertDiagBlocksLowerTriangular" | custom-call | tf_op jit(solution)/shard_map/jit(_cho_solve)/triangular_solve | solution.py:81
  372.4 0.4 fusion.6
  372.8 0.6 convolution_subtract_fusion.1
  373.4 0.4 fusion.25
  373.9 0.4 fusion.36
  374.2 0.4 convolution_subtract_fusion
  374.7 0.4 convolution_convert_fusion.3
  375.0 0.7 maximum_bitcast_fusion
  375.8 1.1 copy.71
  376.9 66.5 %all-gather.5.cloned.1.call-done = bf16[16384,256]{0,1:T(8,128)(2,1)} async-done(((bf16[512,256]{0,1:T(8,128)(2,1)}), bf16[16384,256]{0,1:T(8,128)(2,1)}) %all-gather.5.cloned.1.call-update) | async-done | bytes 8388624 | tf_op jit(solution)/shard_map/all_gather | solution.py:25
  443.4 12.0 %copy.92 = bf16[16384,256]{1,0:T(8,128)(2,1)} copy(bf16[16384,256]{0,1:T(8,128)(2,1)} %all-gather.5.cloned.1.call-done) | data formatting | bytes 16777216 | tf_op jit(solution)/shard_map/reshape | solution.py:25
  455.4 5.4 gather_fusion.3
  460.8 4.4 gather_fusion.4
  465.2 5.5 convert_bitcast_fusion
  470.7 6.8 %copy.99 = bf16[8,8,128,256]{3,1,2,0:T(8,128)(2,1)} copy(bf16[8,8,128,256]{2,3,1,0:T(8,128)(2,1)} %bitcast.178) | data formatting | bytes 8388608
  477.5 3.0 convolution_convert_fusion.1
  480.6 1.1 convolution_bitcast_fusion.1
  481.9 112.9 %all-reduce.8.cloned.1.call-done = f32[2,256,256]{1,2,0:T(8,128)} async-done(((f32[2,256,256]{1,2,0:T(8,128)}), f32[2,256,256]{1,2,0:T(8,128)}) %all-reduce.8.cloned.1.call-update) | async-done | bytes 524304 | tf_op jit(solution)/shard_map/psum | solution.py:96
  594.9 1.7 fusion.13
  596.6 0.6 convolution_multiply_fusion
  597.2 0.6 fusion.10
  597.8 1.4 fusion.8
  (55 shorter events, 1.4 us)
Async XLA Ops:
  7.2 16.4 %copy-start = (bf16[1,1,64,128,128]{4,3,2,1,0:T(8,128)(2,1)S(1)}, bf16[1,1,64,128,128]{4,3,2,1,0:T(8,128)(2,1)}, u32[]{:S(2)}) copy-start(bf16[1,1,64,128,128]{4,3,2,1,0:T(8,128)(2,1)} %param.9) | copy-start | bytes 6291460
  7.2 13.6 %copy-start.1 = (bf16[512,256]{1,0:T(8,128)(2,1)S(1)}, bf16[512,256]{1,0:T(8,128)(2,1)}, u32[]{:S(2)}) copy-start(bf16[512,256]{1,0:T(8,128)(2,1)} %param.14) | copy-start | bytes 786436
  7.2 145.9 %all-reduce.6.cloned.1.call-start = ((), (), s32[]{:S(2)}) async-start(), calls=%async_computation.2 | async-start | bytes 524288 | tf_op jit(solution)/shard_map/psum | solution.py:70
  9.4 204.8 %all-gather.3.cloned.1.call-start = ((), (), s32[]{:S(2)}) async-start(), calls=%async_computation.3 | async-start | bytes 8650752 | tf_op jit(solution)/shard_map/all_gather | solution.py:25
  11.5 32.2 %all-to-all-start = ((s32[32,1,1]{2,1,0:T(1,128)}), s32[32,1,1]{2,1,0:T(1,128)S(1)}, u32[]{:S(2)}, u32[]{:S(2)}) async-start(s32[32,1,1]{2,1,0:T(1,128)} %copy.58), calls=%async_computation | async-start | bytes 32768 | tf_op jit(solution)/shard_map/all_to_all | solution.py:22
  29.0 6.8 %copy-start.7 = (s32[1,1,64]{2,1,0:T(1,128)S(1)}, s32[1,1,64]{2,1,0:T(1,128)}, u32[]{:S(2)}) copy-start(s32[1,1,64]{2,1,0:T(1,128)} %param.10) | copy-start | bytes 772
  29.0 6.8 %copy-start.8 = (s32[1,1,64]{2,1,0:T(1,128)S(1)}, s32[1,1,64]{2,1,0:T(1,128)}, u32[]{:S(2)}) copy-start(s32[1,1,64]{2,1,0:T(1,128)} %param.11) | copy-start | bytes 772
  29.0 6.8 %copy-start.10 = (s32[1,1,64]{2,1,0:T(1,128)S(1)}, s32[1,1,64]{2,1,0:T(1,128)}, u32[]{:S(2)}) copy-start(s32[1,1,64]{2,1,0:T(1,128)} %param.12) | copy-start | bytes 772
  39.4 1.1 copy-start.2
  43.8 8.1 %copy-start.9 = (s32[1,1,32,1]{2,3,1,0:T(1,128)S(1)}, s32[1,1,32,1]{2,3,1,0:T(1,128)}, u32[]{:S(2)}) copy-start(s32[1,1,32,1]{2,3,1,0:T(1,128)} %param.13) | copy-start | bytes 388
  43.8 113.8 %all-to-all-start.1 = ((f32[32,1,128,256]{3,2,1,0:T(8,128)}), f32[32,1,128,256]{3,2,1,0:T(8,128)}, u32[]{:S(2)}, u32[]{:S(2)}) async-start(f32[32,1,128,256]{3,2,1,0:T(8,128)} %convolution_bitcast_fusion), calls=%async_computation.1 | async-start | bytes 8388608 | tf_op jit(solution)/shard_map/all_to_all | solution.py:60
  51.3 259.1 %all-reduce.10.cloned.1.call-start = ((), (), s32[]{:S(2)}) async-start(), calls=%async_computation.6 | async-start | bytes 1572864 | tf_op jit(solution)/shard_map/psum | solution.py:78
  240.5 202.9 %all-gather.5.cloned.1.call-start = ((), (), s32[]{:S(2)}) async-start(), calls=%async_computation.4 | async-start | bytes 8650752 | tf_op jit(solution)/shard_map/all_gather | solution.py:25
  310.5 61.9 %copy-start.5 = (f32[256,512]{0,1:T(8,128)S(1)}, f32[256,512]{0,1:T(8,128)}, u32[]{:S(2)}) copy-start(f32[256,512]{0,1:T(8,128)} %get-tuple-element.26) | copy-start | bytes 1572868
  375.8 219.1 %all-reduce.8.cloned.1.call-start = ((), (), s32[]{:S(2)}) async-start(), calls=%async_computation.5 | async-start | bytes 1048576 | tf_op jit(solution)/shard_map/psum | solution.py:96
  376.9 103.7 %copy-start.4 = (bf16[512,256]{1,0:T(8,128)(2,1)}, bf16[512,256]{1,0:T(8,128)(2,1)S(1)}, u32[]{:S(2)}) copy-start(bf16[512,256]{1,0:T(8,128)(2,1)S(1)} %copy.71) | copy-start | bytes 786436
  477.5 4.3 copy-start.6
  477.5 117.4 %copy-start.3 = (f32[256,256]{1,0:T(8,128)S(1)}, f32[256,256]{1,0:T(8,128)}, u32[]{:S(2)}) copy-start(f32[256,256]{1,0:T(8,128)} %param.16) | copy-start | bytes 786436
Sparse Core Ops, SparseCore 0:
  11.8 141.2 all-reduce.5
  156.0 58.1 all-gather.2
  240.7 69.7 all-reduce.9
  375.9 67.4 all-gather.4
  481.9 112.9 all-reduce.7
where the time goes:
time: 613 us; the launch traced here: 606 us
  waiting for transfers between devices  401 us (65%)
  local copies, waits for them, and re-layouts  67.8 us (11%)
  other arithmetic  57.9 us (9%)
  matrix products  46.8 us (8%)
  starting transfers between devices  17 us (3%)
  between operations  15.7 us (3%)
    all_gather x2, waiting for transfers between devices, neighbour(): lax.all_gather(slab_rows, 'ent', axis=0, tiled=True)  117 us
    psum x1, waiting for transfers between devices, shards(): totals = lax.psum(core_part, 'ent')  113 us
    psum x1, waiting for transfers between devices, shards(): lax.psum(jnp.einsum('ar,as->rs', factors, factors, preferred_element_type...  101 us
    psum x1, waiting for transfers between devices, shards(): numerator, system = lax.psum((forward_term + landed, system_part), 'rel')  69.7 us
    another operation x6, other arithmetic, shards(): factor_low = jnp.linalg.cholesky(system)  34 us
    unnamed x30, local copies, waits for them, and re-layouts  27.6 us
    another operation x3, other arithmetic, shards(): jax.scipy.linalg.cho_solve((factor_low, True), numerator.T)  19.7 us
  transfers between devices with their start and end apart: 7, of which 5 were waited for; matrix products, arithmetic and copies ran while one was open for 6% of the time, Pallas kernels for 0%

commit v1 on v0

--- a/solution.py
+++ b/solution.py
@@ -22,9 +22,9 @@
     requests = lax.all_to_all(asked_rows, "ent", split_axis=0, concat_axis=0, tiled=True)
 
     def neighbour(slab_rows):
-        whole_table = lax.all_gather(slab_rows, "ent", axis=0, tiled=True).reshape(
-            count_ent, row_blocks, tile_edge, rank_width
-        )
+        whole_table = jnp.concatenate(
+            lax.all_to_all(jnp.stack([slab_rows] * lax.axis_size("ent")), "ent", 0, 0), axis=0
+        ).reshape(count_ent, row_blocks, tile_edge, rank_width)
         fetched = whole_table[jnp.arange(count_ent)[:, None], asked_rows]
         return fetched.reshape(slot_total, tile_edge, rank_width)[sources]
 

time: 613 us -> 724 us (1.18)
  blocking collectives: 0 us -> 166 us
  waiting for transfers between devices: 401 us -> 357 us
  local copies, waits for them, and re-layouts: 67.8 us -> 59.9 us
    all_to_all x0 -> x2, blocking collectives: none -> 166 us  [the longest x1 107 us: neighbour(): lax.all_to_all(jnp.stack([slab_rows] * lax.axis_size('ent')), 'ent', 0, 0)]
    all_gather x2 -> x0, waiting for transfers between devices: 117 us -> none  [neighbour(): lax.all_gather(slab_rows, 'ent', axis=0, tiled=True)]
    psum x1, waiting for transfers between devices: 101 us -> 177 us  [shards(): lax.psum(jnp.einsum('ar,as->rs', factors, factors, preferred_element_type...]
    reshape x1 -> x0, local copies, waits for them, and re-layouts: 12 us -> none  [neighbour(): lax.all_gather(slab_rows, 'ent', axis=0, tiled=True)]
    unnamed x30 -> x32, local copies, waits for them, and re-layouts: 27.6 us -> 24.4 us
  transfers between devices with their start and end apart: 7 -> 5, of which waited for: 5 -> 3; matrix products, arithmetic and copies ran while one was open for 6% -> 5% of each run, Pallas kernels for 0% -> 0%
where the time goes in v1:
time: 724 us; the launch traced here: 717 us
  waiting for transfers between devices  357 us (49%)
  blocking collectives  166 us (23%)
  local copies, waits for them, and re-layouts  59.9 us (8%)
  other arithmetic  57.2 us (8%)
  matrix products  46.5 us (6%)
  between operations  15.7 us (2%)
  starting transfers between devices  14.4 us (2%)
    psum x1, waiting for transfers between devices, shards(): lax.psum(jnp.einsum('ar,as->rs', factors, factors, preferred_element_type...  177 us
    psum x1, waiting for transfers between devices, shards(): totals = lax.psum(core_part, 'ent')  109 us
    all_to_all x1, blocking collectives, neighbour(): lax.all_to_all(jnp.stack([slab_rows] * lax.axis_size('ent')), 'ent', 0, 0)  107 us
    psum x1, waiting for transfers between devices, shards(): numerator, system = lax.psum((forward_term + landed, system_part), 'rel')  70.3 us
    all_to_all x1, blocking collectives, shards(): lax.all_to_all(backward_term, 'ent', split_axis=0, concat_axis=0, tiled=T...  58.5 us
    another operation x6, other arithmetic, shards(): factor_low = jnp.linalg.cholesky(system)  34 us
    unnamed x32, local copies, waits for them, and re-layouts  24.4 us
    another operation x3, other arithmetic, shards(): jax.scipy.linalg.cho_solve((factor_low, True), numerator.T)  19.7 us
  transfers between devices with their start and end apart: 5, of which 3 were waited for; matrix products, arithmetic and copies ran while one was open for 5% of the time, Pallas kernels for 0%

profile of v1, /device:TPU:1, one launch (start us, length us, event | category | flops | bytes accessed | tf_op | source)
XLA Modules:
  0.0 716.9 jit_solution(9785757245316188803)
XLA Ops:
  7.2 1.5 copy.59
  8.7 8.6 %all-to-all-start.1 = ((s32[32,1,1]{2,1,0:T(1,128)}), s32[32,1,1]{2,1,0:T(1,128)S(1)}, u32[]{:S(2)}, u32[]{:S(2)}) async-start(s32[32,1,1]{2,1,0:T(1,128)} %copy.59), calls=%async_computation.1 | async-start | bytes 32768 | tf_op jit(solution)/shard_map/all_to_all | solution.py:22
  17.3 0.7 fusion.34
  17.9 3.7 gather_fusion.2
  21.7 5.4 convert_bitcast_fusion.1
  27.1 6.8 copy.96
  34.0 3.5 convolution_convert_fusion
  37.6 1.1 copy.97
  38.7 3.2 convolution_bitcast_fusion
  41.9 58.5 %all_to_all.21 = f32[32,1,128,256]{3,2,1,0:T(8,128)} all-to-all(f32[32,1,128,256]{3,2,1,0:T(8,128)} %convolution_bitcast_fusion), channel_id=1, replica_groups=mesh['ent'=32,'rel'=8] {'ent'}, dimensions={0} | all-to-all | bytes 8388608 | tf_op jit(solution)/shard_map/all_to_all | solution.py:60
  100.4 4.2 stack.4
  104.6 5.1 all-to-all-start
  109.7 1.0 fusion.37
  110.7 0.5 all-reduce.10.cloned.1.call-start
  111.3 0.7 reduce.12
  112.0 177.4 %all-reduce.6.cloned.1.call-done = f32[256,256]{1,0:T(8,128)} async-done(((f32[256,256]{1,0:T(8,128)}), f32[256,256]{1,0:T(8,128)}) %all-reduce.6.cloned.1.call-update) | async-done | bytes 262160 | tf_op jit(solution)/shard_map/psum | solution.py:70
  289.3 1.6 fusion.17
  290.9 0.5 convolution_bitcast_fusion.3
  291.4 1.3 fusion.19
  292.7 1.2 fusion.5
  293.9 2.4 copy.98
  296.3 2.3 fusion.31
  298.7 1.4 reshape.238
  300.1 5.4 gather_fusion
  305.5 4.4 gather_fusion.1
  309.9 5.5 convert_bitcast_fusion.2
  315.3 6.8 copy.94
  322.1 2.9 convolution_convert_fusion.2
  325.2 1.1 fusion.4
  326.4 0.2 all-reduce.8.cloned.1.call-start
  326.6 70.3 %all-reduce.10.cloned.1.call-done = (f32[256,512]{0,1:T(8,128)}, f32[256,256]{0,1:T(8,128)}) async-done(((f32[256,512]{0,1:T(8,128)}, f32[256,256]{0,1:T(8,128)}), (f32[256,512]{0,1:T(8,128)}, f32[256,256]{0,1:T(8,128)})) %all-reduce.10.cloned.1.call-update) | async-done | bytes 786448 | tf_op jit(solution)/shard_map/psum | solution.py:78
  396.9 1.0 convert_add_fusion
  398.0 1.0 fusion.16
  399.1 11.7 %cholesky.50 = f32[128,128]{1,0:T(8,128)S(1)} custom-call(f32[128,128]{1,0:T(8,128)S(1)} %cholesky.118), custom_call_target="Cholesky" | custom-call | tf_op jit(solution)/shard_map/jit(cholesky)/cholesky | solution.py:80
  410.8 9.8 %custom-call.18 = f32[1,128,128]{1,2,0:T(8,128)S(1)} custom-call(f32[1,128,128]{2,1,0:T(8,128)S(1)} %get-tuple-element.33), custom_call_target="InvertDiagBlocksLowerTriangular" | custom-call | tf_op jit(solution)/shard_map/jit(cholesky)/cholesky | solution.py:80
  420.6 0.2 constant_dynamic-update-slice_fusion.1
  420.9 0.3 convolution_subtract_fusion.2
  421.1 11.7 %cholesky.105 = f32[128,128]{1,0:T(8,128)S(1)} custom-call(f32[128,128]{1,0:T(8,128)S(1)} %convolution_subtract_fusion.2), custom_call_target="Cholesky" | custom-call | tf_op jit(solution)/shard_map/jit(cholesky)/cholesky | solution.py:80
  432.9 0.6 compare_reduce_fusion
  434.9 4.2 while.1
  435.1 0.6 fusion.70
  435.7 1.4 bitcast_dynamic-update-slice_fusion.2
  437.1 0.6 fusion.70
  437.7 1.4 bitcast_dynamic-update-slice_fusion.2
  439.1 19.7 %custom-call.19 = f32[2,128,128]{1,2,0:T(8,128)S(1)} custom-call(f32[2,128,128]{2,1,0:T(8,128)S(1)} %get-tuple-element.9), custom_call_target="InvertDiagBlocksLowerTriangular" | custom-call | tf_op jit(solution)/shard_map/jit(_cho_solve)/triangular_solve | solution.py:81
  458.8 0.4 fusion.6
  459.2 0.6 convolution_subtract_fusion.1
  459.8 0.4 fusion.25
  460.3 0.4 fusion.36
  460.6 0.4 convolution_subtract_fusion
  461.1 0.4 convolution_convert_fusion.3
  461.6 0.9 stack.5
  462.6 107.4 %all_to_all.22 = bf16[32,512,256]{2,1,0:T(8,128)(2,1)} all-to-all(bf16[32,512,256]{2,1,0:T(8,128)(2,1)S(1)} %stack.5), channel_id=1, replica_groups=mesh['ent'=32,'rel'=8] {'ent'}, dimensions={0} | all-to-all | bytes 16777216 | tf_op jit(solution)/shard_map/all_to_all | solution.py:26
  569.9 5.4 gather_fusion.3
  575.4 4.4 gather_fusion.4
  579.7 5.5 convert_bitcast_fusion
  585.2 6.8 copy.99
  592.0 3.0 convolution_convert_fusion.1
  595.1 1.1 convolution_bitcast_fusion.1
  596.4 109.4 %all-reduce.8.cloned.1.call-done = f32[2,256,256]{1,2,0:T(8,128)} async-done(((f32[2,256,256]{1,2,0:T(8,128)}), f32[2,256,256]{1,2,0:T(8,128)}) %all-reduce.8.cloned.1.call-update) | async-done | bytes 524304 | tf_op jit(solution)/shard_map/psum | solution.py:96
  705.8 1.7 fusion.13
  707.5 0.6 convolution_multiply_fusion
  708.1 0.6 fusion.10
  708.7 1.4 fusion.8
  (54 shorter events, 1.0 us)
Async XLA Ops:
  7.2 14.5 %copy-start = (bf16[1,1,64,128,128]{4,3,2,1,0:T(8,128)(2,1)S(1)}, bf16[1,1,64,128,128]{4,3,2,1,0:T(8,128)(2,1)}, u32[]{:S(2)}) copy-start(bf16[1,1,64,128,128]{4,3,2,1,0:T(8,128)(2,1)} %param.9) | copy-start | bytes 6291460
  8.7 33.2 %all-to-all-start.1 = ((s32[32,1,1]{2,1,0:T(1,128)}), s32[32,1,1]{2,1,0:T(1,128)S(1)}, u32[]{:S(2)}, u32[]{:S(2)}) async-start(s32[32,1,1]{2,1,0:T(1,128)} %copy.59), calls=%async_computation.1 | async-start | bytes 32768 | tf_op jit(solution)/shard_map/all_to_all | solution.py:22
  27.1 6.9 copy-start.8
  27.1 6.9 copy-start.9
  27.1 6.9 copy-start.11
  37.5 1.1 copy-start.3
  41.9 58.5 %copy-start.1 = (bf16[512,256]{1,0:T(8,128)(2,1)S(1)}, bf16[512,256]{1,0:T(8,128)(2,1)}, u32[]{:S(2)}) copy-start(bf16[512,256]{1,0:T(8,128)(2,1)} %param.14) | copy-start | bytes 786436
  104.6 6.6 copy-start.10
  104.6 195.5 %all-to-all-start = ((bf16[32,512,256]{2,1,0:T(8,128)(2,1)}), bf16[32,512,256]{2,1,0:T(8,128)(2,1)}, u32[]{:S(2)}, u32[]{:S(2)}) async-start(bf16[32,512,256]{2,1,0:T(8,128)(2,1)} %stack.4), calls=%async_computation | async-start | bytes 16777216 | tf_op jit(solution)/shard_map/all_to_all | solution.py:26
  109.7 179.7 %all-reduce.6.cloned.1.call-start = ((), (), s32[]{:S(2)}) async-start(), calls=%async_computation.4 | async-start | bytes 524288 | tf_op jit(solution)/shard_map/psum | solution.py:70
  110.7 286.2 %all-reduce.10.cloned.1.call-start = ((), (), s32[]{:S(2)}) async-start(), calls=%async_computation.6 | async-start | bytes 1572864 | tf_op jit(solution)/shard_map/psum | solution.py:78
  289.3 4.6 copy-start.2
  326.4 379.4 %all-reduce.8.cloned.1.call-start = ((), (), s32[]{:S(2)}) async-start(), calls=%async_computation.5 | async-start | bytes 1048576 | tf_op jit(solution)/shard_map/psum | solution.py:96
  396.9 61.9 %copy-start.6 = (f32[256,512]{0,1:T(8,128)S(1)}, f32[256,512]{0,1:T(8,128)}, u32[]{:S(2)}) copy-start(f32[256,512]{0,1:T(8,128)} %get-tuple-element.26) | copy-start | bytes 1572868
  461.6 133.5 %copy-start.5 = (bf16[512,256]{1,0:T(8,128)(2,1)}, bf16[512,256]{1,0:T(8,128)(2,1)S(1)}, u32[]{:S(2)}) copy-start(bf16[512,256]{1,0:T(8,128)(2,1)S(1)} %copy.72) | copy-start | bytes 786436
  592.0 4.3 copy-start.7
  592.0 113.8 %copy-start.4 = (f32[256,256]{1,0:T(8,128)S(1)}, f32[256,256]{1,0:T(8,128)}, u32[]{:S(2)}) copy-start(f32[256,256]{1,0:T(8,128)} %param.16) | copy-start | bytes 786436
Sparse Core Ops, SparseCore 0:
  114.3 175.0 all-reduce.5
  326.5 70.3 all-reduce.9
  596.4 109.3 all-reduce.7
